TPU v7x, 128 devices: a whole 4x4x4 slice. The times are simulated.
128 devices in a mesh: gx: 8 (over z, core), gy: 4 (over x), gz: 4 (over y).
Axes of the slice: x: 4, y: 4, z: 4, core: 2. Of those that a mesh axis runs over, the one named last changes fastest.
Arguments:
- rhs: float32 [8, 131072], P(None, ('gx', 'gy', 'gz')), may hold values from -8 to 8
- row_order: int32 [131072], P(('gx', 'gy', 'gz')), may hold values from 0 to 1023, as said below
- x_top: float32 [2048, 131072], P(None, ('gx', 'gy', 'gz')), may hold values from -0.03125 to 0.03125
- x_outer: float32 [256, 131072], P(None, ('gx', 'gy', 'gz')), may hold values from -0.09375 to 0.09375
- x_mid: float32 [128, 131072], P(None, ('gx', 'gy', 'gz')), may hold values from -0.15625 to 0.15625
- x_leaf: float32 [960, 131072], P(None, ('gx', 'gy', 'gz')), may hold values from -0.125 to 0.125
- live_outer: int32 [8], P('gx'), may hold values from 128 to 256, as said below
- live_mid: int32 [32], P(('gx', 'gy')), may hold values from 64 to 128, as said below
- live_leaf: int32 [128], P(('gx', 'gy', 'gz')), may hold values from 480 to 960, as said below
Outputs:
- solution: float32 [8, 131072], P(None, ('gx', 'gy', 'gz'))
Inputs may be any that keep to these rules, and one draw needn't show every extreme that they name: `row_order`: each aligned block of 1024 entries is a permutation of 0 to 1023. `live_outer`: some node has all 256 columns live, and some node fewer. `live_mid`: some node has all 128 columns live, and some node fewer. `live_leaf`: some device has all 960 columns live, and some device fewer.
All inputs are finite; a program needn't handle non-finite values.
Results may differ from a plain program's by a relative error of at most 0.0003.
Values sent between devices are 32-bit elements; how exact they have to be, the bound alone decides.
A program may use at most 64 MiB of HBM per device.

v0:
```python
import jax
import jax.numpy as jnp
from jax import lax
from jax.sharding import PartitionSpec as P


def collect(ordered, blocks):
    return lax.dot_general(
        ordered,
        blocks,
        (((1,), (1,)), ((), ())),
        precision=lax.Precision.HIGHEST,
        preferred_element_type=jnp.float32,
    )


def spread(weights, blocks):
    return lax.dot_general(
        weights,
        blocks,
        (((1,), (0,)), ((), ())),
        precision=lax.Precision.HIGHEST,
        preferred_element_type=jnp.float32,
    )


def masked(separator_sums, live_count):
    columns = separator_sums.shape[1]
    column_mask = lax.broadcasted_iota(jnp.int32, (1, columns), 1) < live_count[0]
    return jnp.where(column_mask, separator_sums, jnp.float32(0.0))


def local(rhs, row_order, x_top, x_outer, x_mid, x_leaf, live_outer, live_mid, live_leaf):
    ordered = jnp.take(rhs, row_order, axis=1)
    top_part = collect(ordered, x_top)
    outer_part = collect(ordered, x_outer)
    mid_part = collect(ordered, x_mid)
    leaf_part = collect(ordered, x_leaf)
    top_total = lax.psum(top_part, ("gx", "gy", "gz"))
    outer_total = lax.psum(outer_part, ("gy", "gz"))
    mid_total = lax.psum(mid_part, "gz")
    solution = spread(masked(leaf_part, live_leaf), x_leaf)
    solution = solution + spread(masked(mid_total, live_mid), x_mid)
    solution = solution + spread(masked(outer_total, live_outer), x_outer)
    solution = solution + spread(top_total, x_top)
    return solution


def solution(mesh):
    return jax.shard_map(
        local,
        mesh=mesh,
        in_specs=(
            P(None, ("gx", "gy", "gz")),
            P(("gx", "gy", "gz")),
            P(None, ("gx", "gy", "gz")),
            P(None, ("gx", "gy", "gz")),
            P(None, ("gx", "gy", "gz")),
            P(None, ("gx", "gy", "gz")),
            P("gx"),
            P(("gx", "gy")),
            P(("gx", "gy", "gz")),
        ),
        out_specs=P(None, ("gx", "gy", "gz")),
        check_vma=False,
    )
```

profile of v0, /device:TPU:1, one launch (start us, length us, event | category | flops | bytes accessed | tf_op | source)
XLA Modules:
  0.0 178.7 jit_solution(491466548281910263)
XLA Ops:
  6.5 0.0 copy-start
  6.5 0.0 copy-start.1
  6.5 0.0 all-reduce.2.cloned.1.call-start
  6.5 0.8 fusion.20
  7.4 0.7 compare_and_fusion
  8.0 0.9 copy.10
  9.0 2.8 %gather_fusion = f32[1024,8]{1,0:T(8,128)S(1)} fusion(f32[8,1024]{0,1:T(8,128)S(1)} %copy.10, s32[1024]{0:T(1024)S(1)} %fusion.20), kind=kCustom, calls=%fused_computation | custom fusion | bytes 69632 | tf_op jit(solution)/shard_map/jit(_take)/gather | solution.py:34
  11.8 10.3 %fusion.5 = f32[8,2048]{1,0:T(8,128)} fusion(f32[2048,1024]{1,0:T(8,128)} %param.11, f32[1024,8]{1,0:T(8,128)S(1)} %gather_fusion, pred[1024]{0:T(1024)(128)(4,1)S(1)} %compare_and_fusion), kind=kOutput, calls=%fused_computation.10 | convolution fusion | flops 201334784 | bytes 8487936 | tf_op jit(solution)/shard_map/dot_general | solution.py:8
  22.1 0.0 all-reduce.2.cloned.1.call-update
  22.2 0.0 copy-done.1
  22.2 1.1 fusion.2
  23.3 9.5 %psum.21 = f32[8,128]{1,0:T(8,128)S(1)} all-reduce(f32[8,128]{1,0:T(8,128)S(1)} %fusion.2), channel_id=1, replica_groups=mesh['gx'=8,'gy'=4,'gz'=4] {'gz'}, use_global_device_ids=true, to_apply=%region_0.1 | all-reduce | flops 1024 | bytes 8192 | tf_op jit(solution)/shard_map/psum | solution.py:41
  34.1 0.0 copy-done
  34.2 1.1 fusion
  35.3 31.2 %psum.22 = f32[8,256]{1,0:T(8,128)S(1)} all-reduce(f32[8,256]{1,0:T(8,128)S(1)} %fusion), channel_id=1, replica_groups=mesh['gx'=8,'gy'=4,'gz'=4] {'gy','gz'}, use_global_device_ids=true, to_apply=%region_1.2 | all-reduce | flops 2048 | bytes 16384 | tf_op jit(solution)/shard_map/psum | solution.py:40
  67.1 0.4 fusion.17
  67.5 5.8 %convolution_select_fusion = f32[8,960]{1,0:T(8,128)S(1)} fusion(f32[960,1024]{1,0:T(8,128)} %param.14, f32[1024,8]{1,0:T(8,128)S(1)} %gather_fusion, pred[1024]{0:T(1024)(128)(4,1)S(1)} %compare_and_fusion, pred[960]{0:T(1024)(128)(4,1)S(1)} %iota_compare_fusion), kind=kOutput, calls=%fused_computation.4 | convolution fusion | flops 94387712 | bytes 3997632 | tf_op jit(solution)/shard_map/dot_general | solution.py:8
  73.2 4.1 %convolution_add_fusion.2 = f32[8,1024]{1,0:T(8,128)S(1)} fusion(f32[8,1024]{1,0:T(8,128)S(1)} %fusion.17, f32[8,960]{1,0:T(8,128)S(1)} %convolution_select_fusion, f32[960,1024]{1,0:T(8,128)} %param.14), kind=kOutput, calls=%fused_computation.3 | convolution fusion | flops 94380032 | bytes 4028416 | tf_op jit(solution)/shard_map/dot_general | solution.py:18
  77.3 0.6 convolution_add_fusion.1
  77.9 85.8 %all-reduce.2.cloned.1.call-done = f32[8,2048]{1,0:T(8,128)} async-done(((f32[8,2048]{1,0:T(8,128)}), f32[8,2048]{1,0:T(8,128)}) %all-reduce.2.cloned.1.call-update) | async-done | bytes 65552 | tf_op jit(solution)/shard_map/psum | solution.py:39
  163.8 8.1 %convolution_add_fusion = f32[8,1024]{1,0:T(8,128)} fusion(f32[8,1024]{1,0:T(8,128)S(1)} %convolution_add_fusion.1, f32[8,2048]{1,0:T(8,128)} %all-reduce.2.cloned.1.call-done, f32[2048,1024]{1,0:T(8,128)} %param.11), kind=kOutput, calls=%fused_computation.1 | convolution fusion | flops 201334784 | bytes 8519680 | tf_op jit(solution)/shard_map/dot_general | solution.py:18
  (3 shorter events, 0.0 us)
Async XLA Ops:
  6.5 27.6 %copy-start = (f32[256,1024]{1,0:T(8,128)S(1)}, f32[256,1024]{1,0:T(8,128)}, u32[]{:S(2)}) copy-start(f32[256,1024]{1,0:T(8,128)} %param.12) | copy-start | bytes 3145732
  6.5 15.6 %copy-start.1 = (f32[128,1024]{1,0:T(8,128)S(1)}, f32[128,1024]{1,0:T(8,128)}, u32[]{:S(2)}) copy-start(f32[128,1024]{1,0:T(8,128)} %param.13) | copy-start | bytes 1572868
  6.5 157.2 %all-reduce.2.cloned.1.call-start = ((), (), s32[]{:S(2)}) async-start(), calls=%async_computation | async-start | bytes 131072 | tf_op jit(solution)/shard_map/psum | solution.py:39
Sparse Core Ops, SparseCore 0:
  22.3 141.4 all-reduce.1
where the time goes:
time: 179 us
  waiting for transfers between devices  85.9 us (48%)
  blocking collectives  40.7 us (23%)
  matrix products  31.5 us (18%)
  between operations  15.4 us (9%)
  local copies, waits for them, and re-layouts  3.77 us (2%)
    psum x1, waiting for transfers between devices, local(): top_total = lax.psum(top_part, ('gx', 'gy', 'gz'))  85.8 us
    psum x1, blocking collectives, local(): outer_total = lax.psum(outer_part, ('gy', 'gz'))  31.2 us
    dot_general x4, matrix products, collect(): lax.dot_general(ordered, blocks, (((1,), (1,)), ((), ())), precision=lax....  18.3 us
    dot_general x4, matrix products, spread(): lax.dot_general(weights, blocks, (((1,), (0,)), ((), ())), precision=lax....  13.1 us
    psum x1, blocking collectives, local(): mid_total = lax.psum(mid_part, 'gz')  9.54 us
  transfers between devices with their start and end apart: 1, of which 1 were waited for; matrix products, arithmetic and copies ran while one was open for 7% of the time, Pallas kernels for 0%

commit v1 on v0

v1 whole, which is shorter than its diff:
```python
import jax
import jax.numpy as jnp
from jax import lax
from jax.experimental import pallas as pl
from jax.experimental.pallas import tpu as pltpu
from jax.sharding import PartitionSpec as P

F32 = jnp.float32
BF16 = jnp.bfloat16
LANES = 128
NRHS = 8
ROWS = 1024
CHUNK = 256
TOP = 8
OUTER = 8
MID = 9
LEAF = 10
CHUNKS = 14
PLANE = 16
GX = 8
RING = 4


def halves(values):
    high = values.astype(BF16)
    return high, (values - high.astype(F32)).astype(BF16)


def stacked(values):
    high = values.astype(BF16).astype(F32)
    return jnp.concatenate([high, values - high], axis=0).astype(BF16)


def folded(values):
    return values[:NRHS] + values[NRHS:]


def permuted(rhs, order):
    out = []
    for j in range(ROWS // LANES):
        place = jnp.broadcast_to(order[j : j + 1, :], (NRHS, LANES))
        lane, block = place % LANES, place // LANES
        taken = jnp.zeros((NRHS, LANES), F32)
        for s in range(ROWS // LANES):
            source = rhs[:, s * LANES : (s + 1) * LANES]
            taken = jnp.where(block == s, jnp.take_along_axis(source, lane, axis=1), taken)
        out.append(taken)
    return jnp.concatenate(out, axis=1)


def collect(ordered, blocks):
    return lax.dot_general(ordered, blocks, (((1,), (1,)), ((), ())), preferred_element_type=F32)


def spread(weights, blocks):
    return lax.dot_general(weights, blocks, (((1,), (0,)), ((), ())), preferred_element_type=F32)


def row(pieces):
    return jnp.concatenate(pieces, axis=1)


def live(values, count):
    return jnp.where(lax.broadcasted_iota(jnp.int32, values.shape, 1) < count, values, jnp.float32(0.0))


def kernel(
    rhs_in, order_in, top_in, outer_in, mid_in, leaf_in, live_outer_in, live_mid_in, live_leaf_in, out,
    live_outer, live_mid, live_leaf,
    rhs, order, blocks, split, ordered, part, ring_send, gx_send, top_total,
    plane_recv, gx_recv, mid_recv, outer_recv, outer_send,
    load_sem, small_sem, send_sem, recv_sem,
):
    gx, gy, gz = lax.axis_index("gx"), lax.axis_index("gy"), lax.axis_index("gz")
    me = gy * RING + gz

    def load(chunk):
        return pltpu.make_async_copy(
            top_in.at[pl.ds(chunk * CHUNK, CHUNK)], blocks.at[chunk], load_sem.at[chunk]
        )

    def chunk_of(step):
        return lax.rem(me // 2 + 1 + step, TOP)

    smalls = [
        pltpu.make_async_copy(rhs_in, rhs, small_sem.at[0]),
        pltpu.make_async_copy(order_in, order, small_sem.at[1]),
        pltpu.make_async_copy(live_outer_in, live_outer, small_sem.at[2]),
        pltpu.make_async_copy(live_mid_in, live_mid, small_sem.at[3]),
        pltpu.make_async_copy(live_leaf_in, live_leaf, small_sem.at[4]),
    ]
    for copy in smalls:
        copy.start()

    @pl.loop(0, TOP)
    def _(step):
        load(chunk_of(step)).start()

    rest = [
        pltpu.make_async_copy(outer_in, blocks.at[OUTER], load_sem.at[OUTER]),
        pltpu.make_async_copy(mid_in, blocks.at[MID, pl.ds(0, 128)], load_sem.at[MID]),
    ]
    for i in range(4):
        rows = 256 if i < 3 else 192
        rest.append(
            pltpu.make_async_copy(
                leaf_in.at[pl.ds(i * CHUNK, rows)], blocks.at[LEAF + i, pl.ds(0, rows)], load_sem.at[LEAF + i]
            )
        )
    for copy in rest:
        copy.start()

    barrier = pltpu.get_barrier_semaphore()

    @pl.loop(1, PLANE)
    def _(step):
        other = lax.rem(me + step, PLANE)
        pl.semaphore_signal(barrier, inc=1, device_id={"gy": other // RING, "gz": lax.rem(other, RING)})

    @pl.loop(1, GX)
    def _(step):
        pl.semaphore_signal(barrier, inc=1, device_id={"gx": lax.rem(gx + step, GX)})

    blocks[MID, pl.ds(128, 128)] = jnp.zeros((128, ROWS), F32)
    blocks[LEAF + 3, pl.ds(192, 64)] = jnp.zeros((64, ROWS), F32)
    for copy in smalls:
        copy.wait()
    ordered[...] = stacked(permuted(rhs[...], order[...]))
    pl.semaphore_wait(barrier, PLANE - 1 + GX - 1)

    def gather_sums(chunk):
        high, low = halves(blocks[chunk])
        split[chunk, pl.ds(0, CHUNK)] = high
        split[chunk, pl.ds(CHUNK, CHUNK)] = low
        sums = folded(collect(ordered[...], high) + collect(ordered[...], low))
        part[2 * chunk] = sums[:, :LANES]
        part[2 * chunk + 1] = sums[:, LANES:]

    @pl.loop(0, TOP)
    def _(step):
        chunk = chunk_of(step)
        load(chunk).wait()
        gather_sums(chunk)
        for k in range(2):
            owner = 2 * chunk + k

            @pl.when(owner != me)
            def _():
                pltpu.make_async_remote_copy(
                    src_ref=part.at[owner],
                    dst_ref=plane_recv.at[lax.rem(me - owner + PLANE, PLANE)],
                    send_sem=send_sem.at[0],
                    recv_sem=recv_sem.at[0],
                    device_id={"gy": owner // RING, "gz": lax.rem(owner, RING)},
                ).start()

    rest[0].wait()
    gather_sums(OUTER)
    rest[1].wait()
    gather_sums(MID)
    ring_send[...] = part[pl.ds(2 * OUTER, 3)]
    for step in range(1, RING):
        pltpu.make_async_remote_copy(
            src_ref=ring_send,
            dst_ref=mid_recv.at[RING - step],
            send_sem=send_sem.at[1],
            recv_sem=recv_sem.at[1],
            device_id={"gz": lax.rem(gz + step, RING)},
        ).start()

    def leaf_chunk(i):
        rest[2 + i].wait()
        gather_sums(LEAF + i)

    leaf_chunk(0)
    leaf_chunk(1)

    def wait_for(ref, sem):
        pltpu.make_async_copy(ref, ref, sem).wait()

    wait_for(plane_recv.at[pl.ds(1, PLANE - 1)], recv_sem.at[0])
    gx_send[...] = part[me] + jnp.sum(plane_recv[pl.ds(1, PLANE - 1)], axis=0)
    for step in range(1, GX):
        pltpu.make_async_remote_copy(
            src_ref=gx_send,
            dst_ref=gx_recv.at[GX - step],
            send_sem=send_sem.at[2],
            recv_sem=recv_sem.at[2],
            device_id={"gx": lax.rem(gx + step, GX)},
        ).start()

    leaf_chunk(2)
    leaf_chunk(3)

    wait_for(mid_recv.at[pl.ds(1, RING - 1)], recv_sem.at[1])
    ring_total = ring_send[...] + jnp.sum(mid_recv[pl.ds(1, RING - 1)], axis=0)
    outer_send[...] = ring_total[:2]
    for step in range(1, RING):
        pltpu.make_async_remote_copy(
            src_ref=outer_send,
            dst_ref=outer_recv.at[RING - step],
            send_sem=send_sem.at[3],
            recv_sem=recv_sem.at[3],
            device_id={"gy": lax.rem(gy + step, RING)},
        ).start()

    wait_for(gx_recv.at[pl.ds(1, GX - 1)], recv_sem.at[2])
    top_total[me] = gx_send[...] + jnp.sum(gx_recv[pl.ds(1, GX - 1)], axis=0)

    @pl.loop(1, PLANE)
    def _(step):
        other = lax.rem(me + step, PLANE)
        pltpu.make_async_remote_copy(
            src_ref=top_total.at[me],
            dst_ref=top_total.at[me],
            send_sem=send_sem.at[4],
            recv_sem=recv_sem.at[4],
            device_id={"gy": other // RING, "gz": lax.rem(other, RING)},
        ).start()

    def spread_chunks(first, count, weights):
        doubled = []
        for i in range(count):
            both = stacked(weights[:, i * CHUNK : (i + 1) * CHUNK])
            doubled += [both, both]
        return spread(row(doubled), split[pl.ds(first, count)].reshape(count * 2 * CHUNK, ROWS))

    leaf_weights = live(row([part[2 * LEAF + i] for i in range(8)]), live_leaf[0])
    result = spread_chunks(LEAF, 4, leaf_weights)
    wait_for(outer_recv.at[pl.ds(1, RING - 1)], recv_sem.at[3])
    outer_total = outer_send[...] + jnp.sum(outer_recv[pl.ds(1, RING - 1)], axis=0)
    outer_weights = live(row([outer_total[0], outer_total[1]]), live_outer[0])
    mid_weights = live(row([ring_total[2], jnp.zeros((NRHS, LANES), F32)]), live_mid[0])
    result += spread_chunks(OUTER, 2, row([outer_weights, mid_weights]))

    wait_for(top_total.at[pl.ds(0, PLANE - 1)], recv_sem.at[4])
    result += spread_chunks(0, TOP, row([top_total[i] for i in range(PLANE)]))
    out[...] = folded(result)

    wait_for(plane_recv.at[pl.ds(1, PLANE - 1)], send_sem.at[0])
    wait_for(mid_recv.at[pl.ds(1, RING - 1)], send_sem.at[1])
    wait_for(gx_recv.at[pl.ds(1, GX - 1)], send_sem.at[2])
    wait_for(outer_recv.at[pl.ds(1, RING - 1)], send_sem.at[3])
    wait_for(top_total.at[pl.ds(0, PLANE - 1)], send_sem.at[4])


def local(rhs, row_order, x_top, x_outer, x_mid, x_leaf, live_outer, live_mid, live_leaf):
    piece = (NRHS, LANES)
    call = pl.pallas_call(
        kernel,
        out_shape=jax.ShapeDtypeStruct((NRHS, ROWS), F32),
        in_specs=[pl.BlockSpec(memory_space=pltpu.HBM)] * 6 + [pl.BlockSpec(memory_space=pl.ANY)] * 3,
        out_specs=pl.BlockSpec(memory_space=pltpu.VMEM),
        scratch_shapes=[
            pltpu.SMEM((1,), jnp.int32),
            pltpu.SMEM((1,), jnp.int32),
            pltpu.SMEM((1,), jnp.int32),
            pltpu.VMEM((NRHS, ROWS), F32),
            pltpu.VMEM((ROWS // LANES, LANES), jnp.int32),
            pltpu.VMEM((CHUNKS, CHUNK, ROWS), F32),
            pltpu.VMEM((CHUNKS, 2 * CHUNK, ROWS), BF16),
            pltpu.VMEM((2 * NRHS, ROWS), BF16),
            pltpu.VMEM((2 * CHUNKS, *piece), F32),
            pltpu.VMEM((3, *piece), F32),
            pltpu.VMEM(piece, F32),
            pltpu.VMEM((PLANE, *piece), F32),
            pltpu.VMEM((PLANE, *piece), F32),
            pltpu.VMEM((GX, *piece), F32),
            pltpu.VMEM((RING, 3, *piece), F32),
            pltpu.VMEM((RING, 2, *piece), F32),
            pltpu.VMEM((2, *piece), F32),
            pltpu.SemaphoreType.DMA((CHUNKS,)),
            pltpu.SemaphoreType.DMA((5,)),
            pltpu.SemaphoreType.DMA((5,)),
            pltpu.SemaphoreType.DMA((5,)),
        ],
        compiler_params=pltpu.CompilerParams(
            collective_id=0, has_side_effects=True, vmem_limit_bytes=48 * 1024 * 1024
        ),
        cost_estimate=pl.CostEstimate(flops=2 * 4 * 8 * 1024 * 3392, bytes_accessed=3392 * 4096, transcendentals=0),
        name="xxt",
    )
    large = (rhs, row_order.reshape(ROWS // LANES, LANES), x_top, x_outer, x_mid, x_leaf)
    large = [pltpu.with_memory_space_constraint(operand, pltpu.HBM) for operand in large]
    return call(*large, live_outer, live_mid, live_leaf)


def solution(mesh):
    return jax.shard_map(
        local,
        mesh=mesh,
        in_specs=(
            P(None, ("gx", "gy", "gz")),
            P(("gx", "gy", "gz")),
            P(None, ("gx", "gy", "gz")),
            P(None, ("gx", "gy", "gz")),
            P(None, ("gx", "gy", "gz")),
            P(None, ("gx", "gy", "gz")),
            P("gx"),
            P(("gx", "gy")),
            P(("gx", "gy", "gz")),
        ),
        out_specs=P(None, ("gx", "gy", "gz")),
        check_vma=False,
    )
```

time: 179 us -> 28.1 us (0.16)
  waiting for transfers between devices: 85.9 us -> 0 us
  blocking collectives: 40.7 us -> 0 us
  matrix products: 31.5 us -> 0 us
  Pallas kernels: 0 us -> 25.4 us
  between operations: 15.4 us -> 1.95 us
  local copies, waits for them, and re-layouts: 3.77 us -> 0.62 us
    psum x1 -> x0, waiting for transfers between devices: 85.8 us -> none  [local(): top_total = lax.psum(top_part, ('gx', 'gy', 'gz'))]
    psum x2 -> x0, blocking collectives: 40.7 us -> none  [the longest x1 31.2 us: local(): outer_total = lax.psum(outer_part, ('gy', 'gz'))]
    dot_general x8 -> x0, matrix products: 31.5 us -> none  [the longest x4 18.3 us: collect(): lax.dot_general(ordered, blocks, (((1,), (1,)), ((), ())), precision=lax....]
    pallas_call x0 -> x1, Pallas kernels: none -> 25.4 us  [local(): return call(*large, live_outer, live_mid, live_leaf)]
    gather x1 -> x0, local copies, waits for them, and re-layouts: 2.81 us -> none  [local(): ordered = jnp.take(rhs, row_order, axis=1)]
  transfers between devices with their start and end apart: 1 -> 0, of which waited for: 1 -> 0; matrix products, arithmetic and copies ran while one was open for 7% -> 0% of each run, Pallas kernels for 0% -> 0%
where the time goes in v1:
time: 28.1 us; the launch traced here: 28 us
  Pallas kernels  25.4 us (90%)
  between operations  1.95 us (7%)
  local copies, waits for them, and re-layouts  0.62 us (2%)
    pallas_call x1, Pallas kernels, local(): return call(*large, live_outer, live_mid, live_leaf)  25.4 us
    unnamed x1, local copies, waits for them, and re-layouts  0.62 us

profile of v1, /device:TPU:1, one launch (start us, length us, event | category | flops | bytes accessed | tf_op | source)
XLA Modules:
  0.0 28.0 jit_solution(15214980241768920798)
XLA Ops:
  1.9 25.4 %xxt.1 = f32[8,1024]{1,0:T(8,128)S(1)} custom-call(f32[8,1024]{1,0:T(8,128)} %rhs_in.1, s32[8,128]{1,0:T(8,128)} %bitcast.1, f32[2048,1024]{1,0:T(8,128)} %top_in.1, f32[256,1024]{1,0:T(8,128)} %outer_in.1, f32[128,1024]{1,0:T(8,128)} %mid_in.1, f32[960,1024]{1,0:T(8,128)} %leaf_in.1, s32[1]{0:T(128)S(6)} %copy.11.live_outer_in, s32[1]{0:T(128)S(6)} %copy.12.live_mid_in, ...), custom_call_target="tpu_custom_call" | custom-call | flops 222298112 | bytes 13893632 | tf_op jit(solution)/shard_map/xxt/pallas_call | solution.py:285
  27.3 0.6 %copy.14 = f32[8,1024]{1,0:T(8,128)} copy(f32[8,1024]{1,0:T(8,128)S(1)} %xxt.1) | data formatting | bytes 65536

commit v2 on v1

v2 whole, which is shorter than its diff:
```python
import jax
import jax.numpy as jnp
from jax import lax
from jax.experimental import pallas as pl
from jax.experimental.pallas import tpu as pltpu
from jax.sharding import PartitionSpec as P

F32 = jnp.float32
BF16 = jnp.bfloat16
LANES = 128
NRHS = 8
ROWS = 1024
WIDTH = 512
PIECES = WIDTH // LANES
TOP = 4
MIDDLE = 4
LEAF = 5
CHUNKS = 7
PLANE = 16
GX = 8
RING = 4
LATE = 9
EARLY = 2


def halves(values):
    high = values.astype(BF16)
    return high, (values - high.astype(F32)).astype(BF16)


def stacked(values):
    high = values.astype(BF16).astype(F32)
    return jnp.concatenate([high, values - high], axis=0).astype(BF16)


def folded(values):
    return values[:NRHS] + values[NRHS:]


def permuted(rhs, order):
    out = []
    for j in range(ROWS // LANES):
        place = jnp.broadcast_to(order[j : j + 1, :], (NRHS, LANES))
        lane, block = place % LANES, place // LANES
        taken = jnp.zeros((NRHS, LANES), F32)
        for s in range(ROWS // LANES):
            source = rhs[:, s * LANES : (s + 1) * LANES]
            taken = jnp.where(block == s, jnp.take_along_axis(source, lane, axis=1), taken)
        out.append(taken)
    return jnp.concatenate(out, axis=1)


def collect(ordered, blocks):
    return lax.dot_general(ordered, blocks, (((1,), (1,)), ((), ())), preferred_element_type=F32)


def spread(weights, blocks):
    return lax.dot_general(weights, blocks, (((1,), (0,)), ((), ())), preferred_element_type=F32)


def row(pieces):
    return jnp.concatenate(pieces, axis=1)


def live(values, count):
    return jnp.where(lax.broadcasted_iota(jnp.int32, values.shape, 1) < count, values, jnp.float32(0.0))


def place(piece):
    turn = PLANE - 1 - piece
    inner_y, inner_z = turn // 8, lax.rem(turn // 4, 2)
    far_y, far_z = lax.rem(turn // 2, 2), lax.rem(turn, 2)
    return far_y * (3 - 2 * inner_y) + inner_y, far_z * (3 - 2 * inner_z) + inner_z


def piece_at(gy, gz):
    inner_y, inner_z = lax.rem(gy + 1, RING) // 2, lax.rem(gz + 1, RING) // 2
    return PLANE - 1 - (inner_y * 8 + inner_z * 4 + (gy // 2) * 2 + gz // 2)


def wait_for(ref, sem):
    pltpu.make_async_copy(ref, ref, sem).wait()


def kernel(
    rhs_in, order_in, top_in, outer_in, mid_in, leaf_in, live_outer_in, live_mid_in, live_leaf_in, out,
    live_outer, live_mid, live_leaf,
    rhs, order, blocks, split, ordered, part, ring_send, gx_send, top_total, result,
    plane_recv, gx_recv, mid_recv, outer_recv, outer_send,
    load_sem, small_sem, send_sem, recv_sem, total_sem,
):
    gx, gy, gz = lax.axis_index("gx"), lax.axis_index("gy"), lax.axis_index("gz")
    me = gy * RING + gz
    mine = piece_at(gy, gz)
    smalls = [
        pltpu.make_async_copy(rhs_in, rhs, small_sem.at[0]),
        pltpu.make_async_copy(order_in, order, small_sem.at[1]),
        pltpu.make_async_copy(live_outer_in, live_outer, small_sem.at[2]),
        pltpu.make_async_copy(live_mid_in, live_mid, small_sem.at[3]),
        pltpu.make_async_copy(live_leaf_in, live_leaf, small_sem.at[4]),
    ]
    for copy in smalls:
        copy.start()
    for i in range(TOP):
        pltpu.make_async_copy(top_in.at[pl.ds(i * WIDTH, WIDTH)], blocks.at[i], load_sem.at[i]).start(priority=1)
    rest = [
        pltpu.make_async_copy(outer_in, blocks.at[MIDDLE, pl.ds(0, 256)], load_sem.at[MIDDLE]),
        pltpu.make_async_copy(mid_in, blocks.at[MIDDLE, pl.ds(256, 128)], load_sem.at[CHUNKS]),
        pltpu.make_async_copy(leaf_in.at[pl.ds(0, 512)], blocks.at[LEAF], load_sem.at[LEAF]),
        pltpu.make_async_copy(leaf_in.at[pl.ds(512, 448)], blocks.at[LEAF + 1, pl.ds(0, 448)], load_sem.at[LEAF + 1]),
    ]
    for copy in rest:
        copy.start(priority=1)

    barrier = pltpu.get_barrier_semaphore()

    @pl.loop(1, PLANE)
    def _(step):
        other = lax.rem(me + step, PLANE)
        pl.semaphore_signal(barrier, inc=1, device_id={"gy": other // RING, "gz": lax.rem(other, RING)})

    @pl.loop(1, GX)
    def _(step):
        pl.semaphore_signal(barrier, inc=1, device_id={"gx": lax.rem(gx + step, GX)})

    blocks[MIDDLE, pl.ds(384, 128)] = jnp.zeros((128, ROWS), F32)
    blocks[LEAF + 1, pl.ds(448, 64)] = jnp.zeros((64, ROWS), F32)
    for copy in smalls:
        copy.wait()
    ordered[...] = stacked(permuted(rhs[...], order[...]))

    turn = gy + gz + 2 * (gx // 2)
    late, early = turn >= LATE, turn <= EARLY
    between = jnp.logical_not(late | early)

    def enter():
        pl.semaphore_wait(barrier, PLANE - 1 + GX - 1)


    def send_piece(piece):
        to_y, to_z = place(piece)

        @pl.when(piece != mine)
        def _():
            pltpu.make_async_remote_copy(
                src_ref=part.at[piece],
                dst_ref=plane_recv.at[lax.rem(me - (to_y * RING + to_z) + PLANE, PLANE)],
                send_sem=send_sem.at[0],
                recv_sem=recv_sem.at[0],
                device_id={"gy": to_y, "gz": to_z},
            ).start()

    def send_ring():
        ring_send[...] = part[pl.ds(PIECES * MIDDLE, 3)]
        for step in range(1, RING):
            pltpu.make_async_remote_copy(
                src_ref=ring_send,
                dst_ref=mid_recv.at[RING - step],
                send_sem=send_sem.at[1],
                recv_sem=recv_sem.at[1],
                device_id={"gz": lax.rem(gz + step, RING)},
            ).start()

    def exchange_gx():
        wait_for(plane_recv.at[pl.ds(1, PLANE - 1)], recv_sem.at[0])
        gx_send[...] = part[mine] + jnp.sum(plane_recv[pl.ds(1, PLANE - 1)], axis=0)
        for step in range(1, GX):
            pltpu.make_async_remote_copy(
                src_ref=gx_send,
                dst_ref=gx_recv.at[GX - step],
                send_sem=send_sem.at[2],
                recv_sem=recv_sem.at[2],
                device_id={"gx": lax.rem(gx + step, GX)},
            ).start()

    @pl.loop(0, CHUNKS)
    def _(chunk):
        @pl.when(chunk < TOP)
        def _():
            wait_for(blocks.at[chunk], load_sem.at[chunk])

        @pl.when((chunk == MIDDLE) & between)
        def _():
            enter()
            pl.loop(0, PLANE)(send_piece)

        @pl.when((chunk == LEAF) & late)
        def _():
            exchange_gx()

        @pl.when(chunk == MIDDLE)
        def _():
            rest[0].wait()
            rest[1].wait()

        @pl.when(chunk == LEAF)
        def _():
            rest[2].wait()

        @pl.when(chunk == LEAF + 1)
        def _():
            rest[3].wait()

        high, low = halves(blocks[chunk])
        split[chunk, pl.ds(0, WIDTH)] = high
        split[chunk, pl.ds(WIDTH, WIDTH)] = low
        sums = folded(collect(ordered[...], high) + collect(ordered[...], low))
        for k in range(PIECES):
            part[PIECES * chunk + k] = sums[:, k * LANES : (k + 1) * LANES]

        @pl.when((chunk == 0) & late)
        def _():
            enter()

        @pl.when((chunk < TOP) & late)
        def _():
            for k in range(PIECES):
                send_piece(PIECES * chunk + k)

        @pl.when((chunk == MIDDLE) & jnp.logical_not(early))
        def _():
            send_ring()

    @pl.when(early)
    def _():
        enter()
        pl.loop(0, PLANE)(send_piece)
        send_ring()

    @pl.when(jnp.logical_not(late))
    def _():
        exchange_gx()

    wait_for(mid_recv.at[pl.ds(1, RING - 1)], recv_sem.at[1])
    ring_total = ring_send[...] + jnp.sum(mid_recv[pl.ds(1, RING - 1)], axis=0)
    outer_send[...] = ring_total[:2]
    for step in range(1, RING):
        pltpu.make_async_remote_copy(
            src_ref=outer_send,
            dst_ref=outer_recv.at[RING - step],
            send_sem=send_sem.at[3],
            recv_sem=recv_sem.at[3],
            device_id={"gy": lax.rem(gy + step, RING)},
        ).start()

    def twice(pieces):
        both = stacked(row(pieces))
        return row([both, both])

    leaf_weights = live(row([part[PIECES * LEAF + i] for i in range(2 * PIECES)]), live_leaf[0])
    leaf_weights = [leaf_weights[:, i * LANES : (i + 1) * LANES] for i in range(2 * PIECES)]
    result[...] = spread(
        row([twice(leaf_weights[:PIECES]), twice(leaf_weights[PIECES:])]),
        split[pl.ds(LEAF, 2)].reshape(4 * WIDTH, ROWS),
    )

    wait_for(gx_recv.at[pl.ds(1, GX - 1)], recv_sem.at[2])
    top_total[mine] = gx_send[...] + jnp.sum(gx_recv[pl.ds(1, GX - 1)], axis=0)

    def total_copy(piece, other):
        return pltpu.make_async_remote_copy(
            src_ref=top_total.at[piece],
            dst_ref=top_total.at[piece],
            send_sem=send_sem.at[4],
            recv_sem=total_sem.at[piece],
            device_id={"gy": other // RING, "gz": lax.rem(other, RING)},
        )

    @pl.loop(0, PLANE)
    def _(other):
        @pl.when(other != me)
        def _():
            total_copy(mine, other).start()

    wait_for(outer_recv.at[pl.ds(1, RING - 1)], recv_sem.at[3])
    outer_total = outer_send[...] + jnp.sum(outer_recv[pl.ds(1, RING - 1)], axis=0)
    outer_weights = live(row([outer_total[0], outer_total[1]]), live_outer[0])
    mid_weights = live(ring_total[2], live_mid[0])
    result[...] += spread(
        twice([outer_weights, mid_weights, jnp.zeros((NRHS, LANES), F32)]), split[MIDDLE]
    )

    @pl.loop(0, TOP)
    def _(chunk):
        for k in range(PIECES):
            piece = PIECES * chunk + k

            @pl.when(piece != mine)
            def _():
                total_copy(piece, me).wait_recv()

        result[...] += spread(twice([top_total[PIECES * chunk + k] for k in range(PIECES)]), split[chunk])

    out[...] = folded(result[...])

    wait_for(plane_recv.at[pl.ds(1, PLANE - 1)], send_sem.at[0])
    wait_for(mid_recv.at[pl.ds(1, RING - 1)], send_sem.at[1])
    wait_for(gx_recv.at[pl.ds(1, GX - 1)], send_sem.at[2])
    wait_for(outer_recv.at[pl.ds(1, RING - 1)], send_sem.at[3])
    wait_for(top_total.at[pl.ds(0, PLANE - 1)], send_sem.at[4])


def local(rhs, row_order, x_top, x_outer, x_mid, x_leaf, live_outer, live_mid, live_leaf):
    piece = (NRHS, LANES)
    call = pl.pallas_call(
        kernel,
        out_shape=jax.ShapeDtypeStruct((NRHS, ROWS), F32),
        in_specs=[pl.BlockSpec(memory_space=pltpu.HBM)] * 6 + [pl.BlockSpec(memory_space=pl.ANY)] * 3,
        out_specs=pl.BlockSpec(memory_space=pltpu.VMEM),
        scratch_shapes=[
            pltpu.SMEM((1,), jnp.int32),
            pltpu.SMEM((1,), jnp.int32),
            pltpu.SMEM((1,), jnp.int32),
            pltpu.VMEM((NRHS, ROWS), F32),
            pltpu.VMEM((ROWS // LANES, LANES), jnp.int32),
            pltpu.VMEM((CHUNKS, WIDTH, ROWS), F32),
            pltpu.VMEM((CHUNKS, 2 * WIDTH, ROWS), BF16),
            pltpu.VMEM((2 * NRHS, ROWS), BF16),
            pltpu.VMEM((PIECES * CHUNKS, *piece), F32),
            pltpu.VMEM((3, *piece), F32),
            pltpu.VMEM(piece, F32),
            pltpu.VMEM((PLANE, *piece), F32),
            pltpu.VMEM((2 * NRHS, ROWS), F32),
            pltpu.VMEM((PLANE, *piece), F32),
            pltpu.VMEM((GX, *piece), F32),
            pltpu.VMEM((RING, 3, *piece), F32),
            pltpu.VMEM((RING, 2, *piece), F32),
            pltpu.VMEM((2, *piece), F32),
            pltpu.SemaphoreType.DMA((CHUNKS + 1,)),
            pltpu.SemaphoreType.DMA((5,)),
            pltpu.SemaphoreType.DMA((5,)),
            pltpu.SemaphoreType.DMA((4,)),
            pltpu.SemaphoreType.DMA((PLANE,)),
        ],
        compiler_params=pltpu.CompilerParams(
            collective_id=0, has_side_effects=True, vmem_limit_bytes=48 * 1024 * 1024
        ),
        cost_estimate=pl.CostEstimate(flops=2 * 4 * 8 * 1024 * 3392, bytes_accessed=3392 * 4096, transcendentals=0),
        name="xxt",
    )
    large = (rhs, row_order.reshape(ROWS // LANES, LANES), x_top, x_outer, x_mid, x_leaf)
    large = [pltpu.with_memory_space_constraint(operand, pltpu.HBM) for operand in large]
    return call(*large, live_outer, live_mid, live_leaf)


def solution(mesh):
    return jax.shard_map(
        local,
        mesh=mesh,
        in_specs=(
            P(None, ("gx", "gy", "gz")),
            P(("gx", "gy", "gz")),
            P(None, ("gx", "gy", "gz")),
            P(None, ("gx", "gy", "gz")),
            P(None, ("gx", "gy", "gz")),
            P(None, ("gx", "gy", "gz")),
            P("gx"),
            P(("gx", "gy")),
            P(("gx", "gy", "gz")),
        ),
        out_specs=P(None, ("gx", "gy", "gz")),
        check_vma=False,
    )
```

time: 28.1 us -> 25.7 us (0.915)
  Pallas kernels: 25.4 us -> 23 us
    pallas_call x1, Pallas kernels: 25.4 us -> 23 us  [local(): return call(*large, live_outer, live_mid, live_leaf)]
where the time goes in v2:
time: 25.7 us; the launch traced here: 25.6 us
  Pallas kernels  23 us (89%)
  between operations  1.95 us (8%)
  local copies, waits for them, and re-layouts  0.62 us (2%)
    pallas_call x1, Pallas kernels, local(): return call(*large, live_outer, live_mid, live_leaf)  23 us
    unnamed x1, local copies, waits for them, and re-layouts  0.62 us

profile of v2, /device:TPU:1, one launch (start us, length us, event | category | flops | bytes accessed | tf_op | source)
XLA Modules:
  0.0 25.6 jit_solution(17660448415135528577)
XLA Ops:
  1.9 23.0 %xxt.1 = f32[8,1024]{1,0:T(8,128)S(1)} custom-call(f32[8,1024]{1,0:T(8,128)} %rhs_in.1, s32[8,128]{1,0:T(8,128)} %bitcast.1, f32[2048,1024]{1,0:T(8,128)} %top_in.1, f32[256,1024]{1,0:T(8,128)} %outer_in.1, f32[128,1024]{1,0:T(8,128)} %mid_in.1, f32[960,1024]{1,0:T(8,128)} %leaf_in.1, s32[1]{0:T(128)S(6)} %copy.11.live_outer_in, s32[1]{0:T(128)S(6)} %copy.12.live_mid_in, ...), custom_call_target="tpu_custom_call" | custom-call | flops 222298112 | bytes 13893632 | tf_op jit(solution)/shard_map/xxt/pallas_call | solution.py:343
  24.9 0.6 %copy.14 = f32[8,1024]{1,0:T(8,128)} copy(f32[8,1024]{1,0:T(8,128)S(1)} %xxt.1) | data formatting | bytes 65536

commit v3 on v2

--- a/solution.py
+++ b/solution.py
@@ -12,6 +12,7 @@
 ROWS = 1024
 WIDTH = 512
 PIECES = WIDTH // LANES
+HALF = PIECES // 2
 TOP = 4
 MIDDLE = 4
 LEAF = 5
@@ -20,7 +21,7 @@
 GX = 8
 RING = 4
 LATE = 9
-EARLY = 2
+EARLY = 1
 
 
 def halves(values):
@@ -66,16 +67,14 @@
     return jnp.where(lax.broadcasted_iota(jnp.int32, values.shape, 1) < count, values, jnp.float32(0.0))
 
 
-def place(piece):
-    turn = PLANE - 1 - piece
-    inner_y, inner_z = turn // 8, lax.rem(turn // 4, 2)
-    far_y, far_z = lax.rem(turn // 2, 2), lax.rem(turn, 2)
-    return far_y * (3 - 2 * inner_y) + inner_y, far_z * (3 - 2 * inner_z) + inner_z
-
-
-def piece_at(gy, gz):
-    inner_y, inner_z = lax.rem(gy + 1, RING) // 2, lax.rem(gz + 1, RING) // 2
-    return PLANE - 1 - (inner_y * 8 + inner_z * 4 + (gy // 2) * 2 + gz // 2)
+def depth_of(chunk):
+    high, low = chunk // 2, lax.rem(chunk, 2)
+    return 2 - low + high - 2 * high * low
+
+
+def chunk_of(depth):
+    high, low = depth // 2, lax.rem(depth, 2)
+    return 3 - 2 * low - 3 * high + 4 * high * low
 
 
 def wait_for(ref, sem):
@@ -85,13 +84,14 @@
 def kernel(
     rhs_in, order_in, top_in, outer_in, mid_in, leaf_in, live_outer_in, live_mid_in, live_leaf_in, out,
     live_outer, live_mid, live_leaf,
-    rhs, order, blocks, split, ordered, part, ring_send, gx_send, top_total, result,
-    plane_recv, gx_recv, mid_recv, outer_recv, outer_send,
+    rhs, order, blocks, split, ordered, part, weights, result,
+    gx_recv, plane_recv, ring_send, mid_recv, ring_total, outer_recv,
     load_sem, small_sem, send_sem, recv_sem, total_sem,
 ):
     gx, gy, gz = lax.axis_index("gx"), lax.axis_index("gy"), lax.axis_index("gz")
     me = gy * RING + gz
-    mine = piece_at(gy, gz)
+    depth, core = gx // 2, lax.rem(gx, 2)
+    mine = PIECES * chunk_of(depth) + HALF * core
     smalls = [
         pltpu.make_async_copy(rhs_in, rhs, small_sem.at[0]),
         pltpu.make_async_copy(order_in, order, small_sem.at[1]),
@@ -129,26 +129,26 @@
         copy.wait()
     ordered[...] = stacked(permuted(rhs[...], order[...]))
 
-    turn = gy + gz + 2 * (gx // 2)
+    turn = gy + gz + 2 * depth
     late, early = turn >= LATE, turn <= EARLY
     between = jnp.logical_not(late | early)
 
     def enter():
         pl.semaphore_wait(barrier, PLANE - 1 + GX - 1)
 
-
-    def send_piece(piece):
-        to_y, to_z = place(piece)
-
-        @pl.when(piece != mine)
-        def _():
-            pltpu.make_async_remote_copy(
-                src_ref=part.at[piece],
-                dst_ref=plane_recv.at[lax.rem(me - (to_y * RING + to_z) + PLANE, PLANE)],
-                send_sem=send_sem.at[0],
-                recv_sem=recv_sem.at[0],
-                device_id={"gy": to_y, "gz": to_z},
-            ).start()
+    def send_chunk(chunk):
+        for k in range(2):
+            owner = 2 * depth_of(chunk) + k
+
+            @pl.when(owner != gx)
+            def _():
+                pltpu.make_async_remote_copy(
+                    src_ref=part.at[pl.ds(PIECES * chunk + HALF * k, HALF)],
+                    dst_ref=gx_recv.at[lax.rem(gx - owner + GX, GX)],
+                    send_sem=send_sem.at[0],
+                    recv_sem=recv_sem.at[0],
+                    device_id={"gx": owner},
+                ).start()
 
     def send_ring():
         ring_send[...] = part[pl.ds(PIECES * MIDDLE, 3)]
@@ -161,17 +161,37 @@
                 device_id={"gz": lax.rem(gz + step, RING)},
             ).start()
 
-    def exchange_gx():
-        wait_for(plane_recv.at[pl.ds(1, PLANE - 1)], recv_sem.at[0])
-        gx_send[...] = part[mine] + jnp.sum(plane_recv[pl.ds(1, PLANE - 1)], axis=0)
-        for step in range(1, GX):
+    def exchange_plane():
+        wait_for(gx_recv.at[pl.ds(1, GX - 1)], recv_sem.at[0])
+        plane_recv[me] = part[pl.ds(mine, HALF)] + jnp.sum(gx_recv[pl.ds(1, GX - 1)], axis=0)
+
+        @pl.loop(0, PLANE)
+        def _(other):
+            @pl.when(other != me)
+            def _():
+                pltpu.make_async_remote_copy(
+                    src_ref=plane_recv.at[me],
+                    dst_ref=plane_recv.at[me],
+                    send_sem=send_sem.at[2],
+                    recv_sem=recv_sem.at[2],
+                    device_id={"gy": other // RING, "gz": lax.rem(other, RING)},
+                ).start()
+
+    def exchange_gy():
+        wait_for(mid_recv.at[pl.ds(1, RING - 1)], recv_sem.at[1])
+        ring_total[...] = ring_send[...] + jnp.sum(mid_recv[pl.ds(1, RING - 1)], axis=0)
+        for step in range(1, RING):
             pltpu.make_async_remote_copy(
-                src_ref=gx_send,
-                dst_ref=gx_recv.at[GX - step],
-                send_sem=send_sem.at[2],
-                recv_sem=recv_sem.at[2],
-                device_id={"gx": lax.rem(gx + step, GX)},
+                src_ref=ring_total.at[pl.ds(0, 2)],
+                dst_ref=outer_recv.at[RING - step],
+                send_sem=send_sem.at[3],
+                recv_sem=recv_sem.at[3],
+                device_id={"gy": lax.rem(gy + step, RING)},
             ).start()
+
+    def after_top():
+        exchange_plane()
+        pl.when(depth < RING - 1)(exchange_gy)
 
     @pl.loop(0, CHUNKS)
     def _(chunk):
@@ -182,11 +202,11 @@
         @pl.when((chunk == MIDDLE) & between)
         def _():
             enter()
-            pl.loop(0, PLANE)(send_piece)
-
-        @pl.when((chunk == LEAF) & late)
-        def _():
-            exchange_gx()
+            pl.loop(0, TOP)(send_chunk)
+
+        @pl.when((chunk == LEAF) & jnp.logical_not(early))
+        def _():
+            after_top()
 
         @pl.when(chunk == MIDDLE)
         def _():
@@ -214,8 +234,7 @@
 
         @pl.when((chunk < TOP) & late)
         def _():
-            for k in range(PIECES):
-                send_piece(PIECES * chunk + k)
+            send_chunk(chunk)
 
         @pl.when((chunk == MIDDLE) & jnp.logical_not(early))
         def _():
@@ -224,24 +243,9 @@
     @pl.when(early)
     def _():
         enter()
-        pl.loop(0, PLANE)(send_piece)
+        pl.loop(0, TOP)(send_chunk)
         send_ring()
-
-    @pl.when(jnp.logical_not(late))
-    def _():
-        exchange_gx()
-
-    wait_for(mid_recv.at[pl.ds(1, RING - 1)], recv_sem.at[1])
-    ring_total = ring_send[...] + jnp.sum(mid_recv[pl.ds(1, RING - 1)], axis=0)
-    outer_send[...] = ring_total[:2]
-    for step in range(1, RING):
-        pltpu.make_async_remote_copy(
-            src_ref=outer_send,
-            dst_ref=outer_recv.at[RING - step],
-            send_sem=send_sem.at[3],
-            recv_sem=recv_sem.at[3],
-            device_id={"gy": lax.rem(gy + step, RING)},
-        ).start()
+        after_top()
 
     def twice(pieces):
         both = stacked(row(pieces))
@@ -254,50 +258,69 @@
         split[pl.ds(LEAF, 2)].reshape(4 * WIDTH, ROWS),
     )
 
-    wait_for(gx_recv.at[pl.ds(1, GX - 1)], recv_sem.at[2])
-    top_total[mine] = gx_send[...] + jnp.sum(gx_recv[pl.ds(1, GX - 1)], axis=0)
-
-    def total_copy(piece, other):
+    def total_copy(owner, other):
+        piece = PIECES * chunk_of(owner // 2) + HALF * lax.rem(owner, 2)
+        pieces = weights.at[pl.ds(piece, HALF)]
         return pltpu.make_async_remote_copy(
-            src_ref=top_total.at[piece],
-            dst_ref=top_total.at[piece],
+            src_ref=pieces,
+            dst_ref=pieces,
             send_sem=send_sem.at[4],
-            recv_sem=total_sem.at[piece],
-            device_id={"gy": other // RING, "gz": lax.rem(other, RING)},
+            recv_sem=total_sem.at[owner],
+            device_id={"gx": other},
         )
 
-    @pl.loop(0, PLANE)
-    def _(other):
-        @pl.when(other != me)
-        def _():
-            total_copy(mine, other).start()
-
-    wait_for(outer_recv.at[pl.ds(1, RING - 1)], recv_sem.at[3])
-    outer_total = outer_send[...] + jnp.sum(outer_recv[pl.ds(1, RING - 1)], axis=0)
-    outer_weights = live(row([outer_total[0], outer_total[1]]), live_outer[0])
-    mid_weights = live(ring_total[2], live_mid[0])
-    result[...] += spread(
-        twice([outer_weights, mid_weights, jnp.zeros((NRHS, LANES), F32)]), split[MIDDLE]
-    )
-
-    @pl.loop(0, TOP)
-    def _(chunk):
-        for k in range(PIECES):
-            piece = PIECES * chunk + k
-
-            @pl.when(piece != mine)
+    def exchange_total():
+        wait_for(plane_recv.at[pl.ds(0, PLANE - 1)], recv_sem.at[2])
+        weights[pl.ds(mine, HALF)] = jnp.sum(plane_recv[...], axis=0)
+        for other in range(GX):
+
+            @pl.when(gx != other)
             def _():
-                total_copy(piece, me).wait_recv()
-
-        result[...] += spread(twice([top_total[PIECES * chunk + k] for k in range(PIECES)]), split[chunk])
+                total_copy(gx, other).start()
+
+    first = 1 - (depth + RING - 1) // RING
+
+    @pl.loop(0, TOP + 1)
+    def _(step):
+        after = [(step + TOP - k) // TOP for k in range(TOP + 1)]
+        chunk = step + first * (TOP - after[1] - 2 * after[2] - after[3] + 2 * after[4] - step)
+
+        @pl.when(((step == 0) & (depth > 0)) | ((step == 1) & (depth == 0)))
+        def _():
+            exchange_total()
+
+        @pl.when((step == 0) & (depth == RING - 1))
+        def _():
+            exchange_gy()
+
+        @pl.when(chunk < TOP)
+        def _():
+            for k in range(2):
+                owner = 2 * depth_of(chunk) + k
+
+                @pl.when(owner != gx)
+                def _():
+                    total_copy(owner, gx).wait_recv()
+
+        @pl.when(chunk == MIDDLE)
+        def _():
+            wait_for(outer_recv.at[pl.ds(1, RING - 1)], recv_sem.at[3])
+            outer_total = ring_total[pl.ds(0, 2)] + jnp.sum(outer_recv[pl.ds(1, RING - 1)], axis=0)
+            outer_weights = live(row([outer_total[0], outer_total[1]]), live_outer[0])
+            weights[PIECES * MIDDLE] = outer_weights[:, :LANES]
+            weights[PIECES * MIDDLE + 1] = outer_weights[:, LANES:]
+            weights[PIECES * MIDDLE + 2] = live(ring_total[2], live_mid[0])
+            weights[PIECES * MIDDLE + 3] = jnp.zeros((NRHS, LANES), F32)
+
+        result[...] += spread(twice([weights[PIECES * chunk + k] for k in range(PIECES)]), split[chunk])
 
     out[...] = folded(result[...])
 
-    wait_for(plane_recv.at[pl.ds(1, PLANE - 1)], send_sem.at[0])
+    wait_for(gx_recv.at[pl.ds(1, GX - 1)], send_sem.at[0])
     wait_for(mid_recv.at[pl.ds(1, RING - 1)], send_sem.at[1])
-    wait_for(gx_recv.at[pl.ds(1, GX - 1)], send_sem.at[2])
+    wait_for(plane_recv.at[pl.ds(0, PLANE - 1)], send_sem.at[2])
     wait_for(outer_recv.at[pl.ds(1, RING - 1)], send_sem.at[3])
-    wait_for(top_total.at[pl.ds(0, PLANE - 1)], send_sem.at[4])
+    wait_for(gx_recv.at[pl.ds(1, GX - 1)], send_sem.at[4])
 
 
 def local(rhs, row_order, x_top, x_outer, x_mid, x_leaf, live_outer, live_mid, live_leaf):
@@ -317,20 +340,19 @@
             pltpu.VMEM((CHUNKS, 2 * WIDTH, ROWS), BF16),
             pltpu.VMEM((2 * NRHS, ROWS), BF16),
             pltpu.VMEM((PIECES * CHUNKS, *piece), F32),
+            pltpu.VMEM((PIECES * (TOP + 1), *piece), F32),
+            pltpu.VMEM((2 * NRHS, ROWS), F32),
+            pltpu.VMEM((GX, HALF, *piece), F32),
+            pltpu.VMEM((PLANE, HALF, *piece), F32),
             pltpu.VMEM((3, *piece), F32),
-            pltpu.VMEM(piece, F32),
-            pltpu.VMEM((PLANE, *piece), F32),
-            pltpu.VMEM((2 * NRHS, ROWS), F32),
-            pltpu.VMEM((PLANE, *piece), F32),
-            pltpu.VMEM((GX, *piece), F32),
             pltpu.VMEM((RING, 3, *piece), F32),
+            pltpu.VMEM((3, *piece), F32),
             pltpu.VMEM((RING, 2, *piece), F32),
-            pltpu.VMEM((2, *piece), F32),
             pltpu.SemaphoreType.DMA((CHUNKS + 1,)),
             pltpu.SemaphoreType.DMA((5,)),
             pltpu.SemaphoreType.DMA((5,)),
             pltpu.SemaphoreType.DMA((4,)),
-            pltpu.SemaphoreType.DMA((PLANE,)),
+            pltpu.SemaphoreType.DMA((GX,)),
         ],
         compiler_params=pltpu.CompilerParams(
             collective_id=0, has_side_effects=True, vmem_limit_bytes=48 * 1024 * 1024

time: 25.7 us -> 24.6 us (0.957)
  Pallas kernels: 23 us -> 21.9 us
    pallas_call x1, Pallas kernels: 23 us -> 21.9 us  [local(): return call(*large, live_outer, live_mid, live_leaf)]
where the time goes in v3:
time: 24.6 us; the launch traced here: 24.4 us
  Pallas kernels  21.9 us (89%)
  between operations  1.95 us (8%)
  local copies, waits for them, and re-layouts  0.62 us (3%)
    pallas_call x1, Pallas kernels, local(): return call(*large, live_outer, live_mid, live_leaf)  21.9 us
    unnamed x1, local copies, waits for them, and re-layouts  0.62 us

profile of v3, /device:TPU:1, one launch (start us, length us, event | category | flops | bytes accessed | tf_op | source)
XLA Modules:
  0.0 24.4 jit_solution(3161555765075702119)
XLA Ops:
  1.9 21.9 %xxt.1 = f32[8,1024]{1,0:T(8,128)S(1)} custom-call(f32[8,1024]{1,0:T(8,128)} %rhs_in.1, s32[8,128]{1,0:T(8,128)} %bitcast.1, f32[2048,1024]{1,0:T(8,128)} %top_in.1, f32[256,1024]{1,0:T(8,128)} %outer_in.1, f32[128,1024]{1,0:T(8,128)} %mid_in.1, f32[960,1024]{1,0:T(8,128)} %leaf_in.1, s32[1]{0:T(128)S(6)} %copy.11.live_outer_in, s32[1]{0:T(128)S(6)} %copy.12.live_mid_in, ...), custom_call_target="tpu_custom_call" | custom-call | flops 222298112 | bytes 13893632 | tf_op jit(solution)/shard_map/xxt/pallas_call | solution.py:365
  23.8 0.6 %copy.14 = f32[8,1024]{1,0:T(8,128)} copy(f32[8,1024]{1,0:T(8,128)S(1)} %xxt.1) | data formatting | bytes 65536

commit v4 on v3

--- a/solution.py
+++ b/solution.py
@@ -13,6 +13,7 @@
 WIDTH = 512
 PIECES = WIDTH // LANES
 HALF = PIECES // 2
+SIDE = WIDTH // 2
 TOP = 4
 MIDDLE = 4
 LEAF = 5
@@ -101,7 +102,15 @@
     ]
     for copy in smalls:
         copy.start()
-    for i in range(TOP):
+    edges = [
+        pltpu.make_async_copy(
+            top_in.at[pl.ds(i * SIDE, SIDE)], blocks.at[0, pl.ds(i * SIDE, SIDE)], load_sem.at[CHUNKS + 1 + i]
+        )
+        for i in range(2)
+    ]
+    for copy in edges:
+        copy.start(priority=1)
+    for i in range(1, TOP):
         pltpu.make_async_copy(top_in.at[pl.ds(i * WIDTH, WIDTH)], blocks.at[i], load_sem.at[i]).start(priority=1)
     rest = [
         pltpu.make_async_copy(outer_in, blocks.at[MIDDLE, pl.ds(0, 256)], load_sem.at[MIDDLE]),
@@ -132,23 +141,27 @@
     turn = gy + gz + 2 * depth
     late, early = turn >= LATE, turn <= EARLY
     between = jnp.logical_not(late | early)
+    last = depth == RING - 1
 
     def enter():
         pl.semaphore_wait(barrier, PLANE - 1 + GX - 1)
 
+    def send_half(chunk, k):
+        owner = 2 * depth_of(chunk) + k
+
+        @pl.when(owner != gx)
+        def _():
+            pltpu.make_async_remote_copy(
+                src_ref=part.at[pl.ds(PIECES * chunk + HALF * k, HALF)],
+                dst_ref=gx_recv.at[lax.rem(gx - owner + GX, GX)],
+                send_sem=send_sem.at[0],
+                recv_sem=recv_sem.at[0],
+                device_id={"gx": owner},
+            ).start()
+
     def send_chunk(chunk):
-        for k in range(2):
-            owner = 2 * depth_of(chunk) + k
-
-            @pl.when(owner != gx)
-            def _():
-                pltpu.make_async_remote_copy(
-                    src_ref=part.at[pl.ds(PIECES * chunk + HALF * k, HALF)],
-                    dst_ref=gx_recv.at[lax.rem(gx - owner + GX, GX)],
-                    send_sem=send_sem.at[0],
-                    recv_sem=recv_sem.at[0],
-                    device_id={"gx": owner},
-                ).start()
+        send_half(chunk, 0)
+        send_half(chunk, 1)
 
     def send_ring():
         ring_send[...] = part[pl.ds(PIECES * MIDDLE, 3)]
@@ -193,9 +206,20 @@
         exchange_plane()
         pl.when(depth < RING - 1)(exchange_gy)
 
+    def gather_sums(chunk, start, width):
+        high, low = halves(blocks[chunk, pl.ds(start, width)])
+        split[chunk, pl.ds(start, width)] = high
+        split[chunk, pl.ds(WIDTH + start, width)] = low
+        sums = folded(collect(ordered[...], high) + collect(ordered[...], low))
+        for k in range(width // LANES):
+            part[PIECES * chunk + start // LANES + k] = sums[:, k * LANES : (k + 1) * LANES]
+
+    edges[0].wait()
+    gather_sums(0, 0, SIDE)
+
     @pl.loop(0, CHUNKS)
     def _(chunk):
-        @pl.when(chunk < TOP)
+        @pl.when((chunk > 0) & (chunk < TOP))
         def _():
             wait_for(blocks.at[chunk], load_sem.at[chunk])
 
@@ -204,7 +228,11 @@
             enter()
             pl.loop(0, TOP)(send_chunk)
 
-        @pl.when((chunk == LEAF) & jnp.logical_not(early))
+        @pl.when((chunk == MIDDLE) & last)
+        def _():
+            exchange_plane()
+
+        @pl.when((chunk == LEAF) & jnp.logical_not(early | last))
         def _():
             after_top()
 
@@ -221,12 +249,14 @@
         def _():
             rest[3].wait()
 
-        high, low = halves(blocks[chunk])
-        split[chunk, pl.ds(0, WIDTH)] = high
-        split[chunk, pl.ds(WIDTH, WIDTH)] = low
-        sums = folded(collect(ordered[...], high) + collect(ordered[...], low))
-        for k in range(PIECES):
-            part[PIECES * chunk + k] = sums[:, k * LANES : (k + 1) * LANES]
+        @pl.when(chunk > 0)
+        def _():
+            gather_sums(chunk, 0, WIDTH)
+
+        @pl.when(chunk == 0)
+        def _():
+            edges[1].wait()
+            gather_sums(0, SIDE, SIDE)
 
         @pl.when((chunk == 0) & late)
         def _():
@@ -283,7 +313,7 @@
     @pl.loop(0, TOP + 1)
     def _(step):
         after = [(step + TOP - k) // TOP for k in range(TOP + 1)]
-        chunk = step + first * (TOP - after[1] - 2 * after[2] - after[3] + 2 * after[4] - step)
+        chunk = step + first * (TOP - after[1] - 3 * after[2] + after[3] + after[4] - step)
 
         @pl.when(((step == 0) & (depth > 0)) | ((step == 1) & (depth == 0)))
         def _():
@@ -348,7 +378,7 @@
             pltpu.VMEM((RING, 3, *piece), F32),
             pltpu.VMEM((3, *piece), F32),
             pltpu.VMEM((RING, 2, *piece), F32),
-            pltpu.SemaphoreType.DMA((CHUNKS + 1,)),
+            pltpu.SemaphoreType.DMA((CHUNKS + 3,)),
             pltpu.SemaphoreType.DMA((5,)),
             pltpu.SemaphoreType.DMA((5,)),
             pltpu.SemaphoreType.DMA((4,)),

time: 24.6 us -> 24.5 us (level)
  no operation moved by 1% of the time
where the time goes in v4:
time: 24.5 us; the launch traced here: 24.3 us
  Pallas kernels  21.8 us (89%)
  between operations  1.95 us (8%)
  local copies, waits for them, and re-layouts  0.62 us (3%)
    pallas_call x1, Pallas kernels, local(): return call(*large, live_outer, live_mid, live_leaf)  21.8 us
    unnamed x1, local copies, waits for them, and re-layouts  0.62 us

profile of v4, /device:TPU:1, one launch (start us, length us, event | category | flops | bytes accessed | tf_op | source)
XLA Modules:
  0.0 24.3 jit_solution(16389353442435148621)
XLA Ops:
  1.9 21.8 %xxt.1 = f32[8,1024]{1,0:T(8,128)S(1)} custom-call(f32[8,1024]{1,0:T(8,128)} %rhs_in.1, s32[8,128]{1,0:T(8,128)} %bitcast.1, f32[2048,1024]{1,0:T(8,128)} %top_in.1, f32[256,1024]{1,0:T(8,128)} %outer_in.1, f32[128,1024]{1,0:T(8,128)} %mid_in.1, f32[960,1024]{1,0:T(8,128)} %leaf_in.1, s32[1]{0:T(128)S(6)} %copy.11.live_outer_in, s32[1]{0:T(128)S(6)} %copy.12.live_mid_in, ...), custom_call_target="tpu_custom_call" | custom-call | flops 222298112 | bytes 13893632 | tf_op jit(solution)/shard_map/xxt/pallas_call | solution.py:395
  23.7 0.6 %copy.14 = f32[8,1024]{1,0:T(8,128)} copy(f32[8,1024]{1,0:T(8,128)S(1)} %xxt.1) | data formatting | bytes 65536

commit v5 on v4

--- a/solution.py
+++ b/solution.py
@@ -21,7 +21,8 @@
 PLANE = 16
 GX = 8
 RING = 4
-LATE = 9
+LATE = 5
+LATEST = 11
 EARLY = 1
 
 
@@ -141,6 +142,7 @@
     turn = gy + gz + 2 * depth
     late, early = turn >= LATE, turn <= EARLY
     between = jnp.logical_not(late | early)
+    latest = turn >= LATEST
     last = depth == RING - 1
 
     def enter():
@@ -258,11 +260,16 @@
             edges[1].wait()
             gather_sums(0, SIDE, SIDE)
 
-        @pl.when((chunk == 0) & late)
+        @pl.when((chunk == 0) & latest)
         def _():
             enter()
 
-        @pl.when((chunk < TOP) & late)
+        @pl.when((chunk == 1) & late & jnp.logical_not(latest))
+        def _():
+            enter()
+            send_chunk(0)
+
+        @pl.when((chunk < TOP) & late & ((chunk > 0) | latest))
         def _():
             send_chunk(chunk)
 

time: 24.5 us -> 24.4 us (level)
  no operation moved by 1% of the time
where the time goes in v5:
time: 24.4 us; the launch traced here: 24.3 us
  Pallas kernels  21.7 us (89%)
  between operations  1.95 us (8%)
  local copies, waits for them, and re-layouts  0.62 us (3%)
    pallas_call x1, Pallas kernels, local(): return call(*large, live_outer, live_mid, live_leaf)  21.7 us
    unnamed x1, local copies, waits for them, and re-layouts  0.62 us

profile of v5, /device:TPU:1, one launch (start us, length us, event | category | flops | bytes accessed | tf_op | source)
XLA Modules:
  0.0 24.3 jit_solution(9400662303251898559)
XLA Ops:
  1.9 21.7 %xxt.1 = f32[8,1024]{1,0:T(8,128)S(1)} custom-call(f32[8,1024]{1,0:T(8,128)} %rhs_in.1, s32[8,128]{1,0:T(8,128)} %bitcast.1, f32[2048,1024]{1,0:T(8,128)} %top_in.1, f32[256,1024]{1,0:T(8,128)} %outer_in.1, f32[128,1024]{1,0:T(8,128)} %mid_in.1, f32[960,1024]{1,0:T(8,128)} %leaf_in.1, s32[1]{0:T(128)S(6)} %copy.11.live_outer_in, s32[1]{0:T(128)S(6)} %copy.12.live_mid_in, ...), custom_call_target="tpu_custom_call" | custom-call | flops 222298112 | bytes 13893632 | tf_op jit(solution)/shard_map/xxt/pallas_call | solution.py:402
  23.6 0.6 %copy.14 = f32[8,1024]{1,0:T(8,128)} copy(f32[8,1024]{1,0:T(8,128)S(1)} %xxt.1) | data formatting | bytes 65536

commit v6 on v5

--- a/solution.py
+++ b/solution.py
@@ -21,7 +21,7 @@
 PLANE = 16
 GX = 8
 RING = 4
-LATE = 5
+LATE = 3
 LATEST = 11
 EARLY = 1
 

time: 24.4 us -> 24.4 us (level)
  no operation moved by 1% of the time
where the time goes in v6:
time: 24.4 us; the launch traced here: 24.3 us
  Pallas kernels  21.7 us (89%)
  between operations  1.95 us (8%)
  local copies, waits for them, and re-layouts  0.62 us (3%)
    pallas_call x1, Pallas kernels, local(): return call(*large, live_outer, live_mid, live_leaf)  21.7 us
    unnamed x1, local copies, waits for them, and re-layouts  0.62 us

profile of v6, /device:TPU:1, one launch (start us, length us, event | category | flops | bytes accessed | tf_op | source)
XLA Modules:
  0.0 24.3 jit_solution(11894078367378084723)
XLA Ops:
  1.9 21.7 %xxt.1 = f32[8,1024]{1,0:T(8,128)S(1)} custom-call(f32[8,1024]{1,0:T(8,128)} %rhs_in.1, s32[8,128]{1,0:T(8,128)} %bitcast.1, f32[2048,1024]{1,0:T(8,128)} %top_in.1, f32[256,1024]{1,0:T(8,128)} %outer_in.1, f32[128,1024]{1,0:T(8,128)} %mid_in.1, f32[960,1024]{1,0:T(8,128)} %leaf_in.1, s32[1]{0:T(128)S(6)} %copy.11.live_outer_in, s32[1]{0:T(128)S(6)} %copy.12.live_mid_in, ...), custom_call_target="tpu_custom_call" | custom-call | flops 222298112 | bytes 13893632 | tf_op jit(solution)/shard_map/xxt/pallas_call | solution.py:402
  23.6 0.6 %copy.14 = f32[8,1024]{1,0:T(8,128)} copy(f32[8,1024]{1,0:T(8,128)S(1)} %xxt.1) | data formatting | bytes 65536
